TPU v7x, 256 devices: a whole 4x4x8 slice. The times are simulated.
256 devices in a mesh: dp: 8 (over z), space: 32 (over y, x, core).
Axes of the slice: x: 4, y: 4, z: 8, core: 2. Of those that a mesh axis runs over, the one named last changes fastest.
Arguments:
- fields: bfloat16 [8, 64, 64, 4096], P('dp', 'space'), may hold values from -6 to 6
- spec_weights: bfloat16 [32, 1024, 64, 128], P(None, ('dp', 'space')), may hold values from -0.75 to 0.75
- local_weight: bfloat16 [64, 64], replicated, may hold values from -0.75 to 0.75
- bias: float32 [64], replicated, may hold values from -3 to 3
- cotangent: bfloat16 [8, 64, 64, 4096], P('dp', 'space'), may hold values from -6 to 6
Outputs:
- output: bfloat16 [8, 64, 64, 4096], P('dp', 'space')
- grad_input: bfloat16 [8, 64, 64, 4096], P('dp', 'space')
- grad_weights: float32 [32, 1024, 64, 128], P(None, ('dp', 'space'))
All inputs are finite; a program needn't handle non-finite values.
Results may differ from a plain program's by a relative error of at most 0.015.
Values may be sent and summed in bfloat16 or wider, within the bound.
A program may use at most 128 MiB of HBM per device.

v0:
```python
import functools
import math

import jax
import jax.numpy as jnp
import ml_dtypes
import numpy as np
from jax import lax
from jax.experimental import pallas as pl
from jax.experimental.pallas import tpu as pltpu
from jax.sharding import PartitionSpec as P

MESH = pl.DeviceIdType.MESH
BF16 = jnp.bfloat16
F32 = jnp.float32

G = 64
M = 32
NS = 32
ND = 8
J = 4
LANES = 128
BLOCKS = 16

NT = (((1,), (1,)), ((), ()))
TN = (((0,), (0,)), ((), ()))


def tables():
    step = 2.0 * math.pi / G
    cell = np.arange(G)
    freq_z = np.arange(M)
    signed = np.where(np.arange(M) < M // 2, np.arange(M), G - M + np.arange(M))
    halves = np.where(freq_z == 0, 1.0, 2.0)
    angle = (freq_z[:, None] * cell[None, :] % G) * step
    z_rows = np.concatenate([np.cos(angle), -np.sin(angle)]) / 8
    z_rows_half = z_rows * np.tile(halves, 2)[:, None]
    four = np.eye(4)
    z_forward = np.kron(four, z_rows)
    z_forward_half = np.kron(four, z_rows_half)
    inv = np.stack([np.cos(angle), -np.sin(angle)], axis=1).reshape(2 * M, G) / 8
    inv_half = inv * np.repeat(halves, 2)[:, None]
    z_inverse = np.kron(four, inv)
    z_inverse_half = np.kron(four, inv_half)
    iy = np.arange(ND)[None, :] * 4 + np.arange(4)[:, None]
    ang_y = (signed[iy][:, :, None] * cell % G) * step
    c, s = np.cos(ang_y) / 8, np.sin(ang_y) / 8
    y_forward = np.stack([np.stack([c, s], -1), np.stack([-s, c], -1)], 1).reshape(64, 128)
    ct, st = c.transpose(2, 0, 1), s.transpose(2, 0, 1)
    y_inverse = np.stack([np.stack([ct, -st], 2), np.stack([st, ct], 2)], 0).reshape(128, 64)
    xs = 2 * np.arange(NS)[None, :] + np.arange(2)[:, None]
    ang_x = (signed[None, :, None] * xs[:, None, :] % G) * step
    c, s = np.cos(ang_x) / 8, np.sin(ang_x) / 8
    x_forward = np.stack([np.stack([c, s], 2), np.stack([-s, c], 2)], 1)
    x_forward = x_forward.reshape(128, 64)
    x_inverse = np.stack([c.transpose(0, 2, 1), s.transpose(0, 2, 1)]).reshape(128, M)
    return [
        t.astype(np.float32).astype(ml_dtypes.bfloat16)
        for t in (
            z_forward, z_forward_half, z_inverse, z_inverse_half,
            y_forward, y_inverse, x_forward, x_inverse,
        )
    ]


def dot(a, b, dims=(((1,), (0,)), ((), ()))):
    return lax.dot_general(a, b, dims, preferred_element_type=F32)


def kernel(
    x_ref, mix_in, mix_back, bias_ref,
    zf, zfh, zi, zih, yf, yi, xf, xi,
    w_hbm, cot_hbm,
    out_hbm, gin_hbm, gw_hbm,
    w_ref, cot_ref, out_ref, gp_ref, gin_ref, gw_ref,
    a_ref, f_ref, v_ref, u_ref, m_ref,
    send_s, recv_s, send_d, recv_d,
    sem_send_s, sem_recv_s, sem_send_d, sem_recv_d, sem_local,
):
    d = lax.axis_index("dp")
    s = lax.axis_index("space")

    w_copy = pltpu.make_async_copy(w_hbm, w_ref, sem_local.at[0])
    w_copy.start()
    cot_copy = pltpu.make_async_copy(cot_hbm, cot_ref, sem_local.at[1])
    cot_copy.start()

    barrier = pltpu.get_barrier_semaphore()

    def greet_space(i, carry):
        pl.semaphore_signal(barrier, inc=1, device_id=(d, lax.rem(s + i, NS)), device_id_type=MESH)
        return carry

    def greet_dp(i, carry):
        pl.semaphore_signal(barrier, inc=1, device_id=(lax.rem(d + i, ND), s), device_id_type=MESH)
        return carry

    lax.fori_loop(1, NS, greet_space, 0)
    lax.fori_loop(1, ND, greet_dp, 0)

    lo = lax.broadcasted_iota(jnp.int32, (1, LANES), 1) < 64

    def swap(v):
        return pltpu.roll(v, 64, 1)

    def exchange_space(n):
        src, dst = send_s.at[n], recv_s.at[n]

        def go(i, carry):
            t = lax.rem(s + i, NS)
            pltpu.make_async_remote_copy(
                src_ref=src.at[t], dst_ref=dst.at[s],
                send_sem=sem_send_s.at[n], recv_sem=sem_recv_s.at[n],
                device_id=(d, t), device_id_type=MESH,
            ).start()
            return carry

        lax.fori_loop(1, NS, go, 0)
        pltpu.make_async_copy(src.at[s], dst.at[s], sem_recv_s.at[n]).start()

    def exchange_dp(n):
        src, dst = send_d.at[n], recv_d.at[n]

        def go(i, carry):
            t = lax.rem(d + i, ND)
            pltpu.make_async_remote_copy(
                src_ref=src.at[t], dst_ref=dst.at[d],
                send_sem=sem_send_d.at[n], recv_sem=sem_recv_d.at[n],
                device_id=(t, s), device_id_type=MESH,
            ).start()
            return carry

        lax.fori_loop(1, ND, go, 0)
        pltpu.make_async_copy(src.at[d], dst.at[d], sem_recv_d.at[n]).start()

    def arrived_space(n):
        pltpu.make_async_copy(recv_s.at[n], recv_s.at[n], sem_recv_s.at[n]).wait()

    def arrived_dp(n):
        pltpu.make_async_copy(recv_d.at[n], recv_d.at[n], sem_recv_d.at[n]).wait()

    def z_forward(block, table, q):
        a_ref[pl.ds(pl.multiple_of(q * 256, 256), 256), :] = dot(table[...], block, NT)

    def y_forward(n):
        def go(izh, carry):
            for pair in range(2):
                parts = [
                    a_ref[pl.ds(izh * 4 + pair * 2 + e, 128, stride=M), :].astype(BF16)
                    for e in range(2)
                ]
                res = dot(yf[...], jnp.concatenate(parts, axis=1)).astype(BF16)
                for e in range(2):
                    for iyl in range(4):
                        send_s[n, iyl * 8 + izh, pair * 2 + e] = res[
                            iyl * 16 : iyl * 16 + 16, e * 128 : e * 128 + 128
                        ]
            return carry

        lax.fori_loop(0, 8, go, 0, unroll=2)

    def x_forward(n_space, n_dp):
        def widen(t, carry):
            f_ref[pl.ds(pl.multiple_of(t * 64, 64), 64), :] = (
                recv_s[n_space, t].reshape(64, LANES).astype(F32)
            )
            return carry

        lax.fori_loop(0, NS, widen, 0, unroll=4)

        def go(dh, carry):
            for pair in range(2):
                parts = []
                for e in range(2):
                    row = (pair * 2 + e) * 16 + dh
                    parts.append(
                        jnp.concatenate(
                            [
                                f_ref[pl.ds(row, NS, stride=64), :],
                                f_ref[pl.ds(row + 8, NS, stride=64), :],
                            ],
                            axis=0,
                        ).astype(BF16)
                    )
                res = dot(xf[...], jnp.concatenate(parts, axis=1))
                for e in range(2):
                    p00, p01, p10, p11 = (
                        res[b * 32 : b * 32 + 32, e * 128 : e * 128 + 128] for b in range(4)
                    )
                    both = jnp.where(lo, p00, p11) + swap(jnp.where(lo, p01, p10))
                    send_d[n_dp, dh, pair * 2 + e] = both.astype(BF16)
            return carry

        lax.fori_loop(0, ND, go, 0, unroll=2)

    def widen_dp(n, to):
        def go(b, carry):
            to[pl.ds(pl.multiple_of(b * 128, 128), 128), :] = (
                recv_d[n, b].reshape(128, LANES).astype(F32)
            )
            return carry

        lax.fori_loop(0, ND, go, 0)

    def narrow_dp(n):
        def go(b, carry):
            send_d[n, b] = (
                m_ref[pl.ds(pl.multiple_of(b * 128, 128), 128), :]
                .astype(BF16)
                .reshape(J, M, LANES)
            )
            return carry

        lax.fori_loop(0, ND, go, 0)

    def x_inverse(n_dp, n_space):
        def go(dh, carry):
            for pair in range(2):
                rhs = jnp.concatenate(
                    [recv_d[n_dp, dh, pair * 2], recv_d[n_dp, dh, pair * 2 + 1]], axis=1
                )
                res = dot(xi[...], rhs)
                for e in range(2):
                    c0, c1, s0, s1 = (
                        res[b * 32 : b * 32 + 32, e * 128 : e * 128 + 128] for b in range(4)
                    )
                    re = jnp.where(lo, c0, -s1) + swap(jnp.where(lo, c1, -s0))
                    im = jnp.where(lo, s0, c1) + swap(jnp.where(lo, s1, c0))
                    row = (pair * 2 + e) * 16 + dh
                    f_ref[pl.ds(row, NS, stride=64), :] = re
                    f_ref[pl.ds(row + 8, NS, stride=64), :] = im
            return carry

        lax.fori_loop(0, ND, go, 0, unroll=2)

        def narrow(t, carry):
            send_s[n_space, t] = (
                f_ref[pl.ds(pl.multiple_of(t * 64, 64), 64), :].astype(BF16).reshape(J, 16, LANES)
            )
            return carry

        lax.fori_loop(0, NS, narrow, 0, unroll=4)

    def y_inverse(n):
        def go(izh, carry):
            for pair in range(2):
                parts = [
                    jnp.concatenate(
                        [recv_s[n, iyl * 8 + izh, pair * 2 + e] for iyl in range(4)], axis=0
                    )
                    for e in range(2)
                ]
                res = dot(yi[...], jnp.concatenate(parts, axis=1))
                for e in range(2):
                    iz = izh * 4 + pair * 2 + e
                    a_ref[pl.ds(pl.multiple_of(iz * 128, 128), 128), :] = res[
                        :, e * 128 : e * 128 + 128
                    ]
            return carry

        lax.fori_loop(0, 8, go, 0, unroll=2)

    def z_inverse(table, q):
        rows = [a_ref[pl.ds(q * 4 + yl, 64, stride=64), :] for yl in range(4)]
        return dot(jnp.concatenate(rows, axis=0).astype(BF16), table[...], TN)

    def first(q, carry):
        cells = pl.ds(pl.multiple_of(q * 256, 256), 256)
        z_forward(x_ref[:, cells], zf, q)
        return carry

    lax.fori_loop(0, BLOCKS, first, 0, unroll=2)
    y_forward(0)
    pl.semaphore_wait(barrier, NS + ND - 2)
    exchange_space(0)
    arrived_space(0)
    x_forward(0, 0)
    exchange_dp(0)
    w_copy.wait()
    arrived_dp(0)

    widen_dp(0, v_ref)
    sign = jnp.where(lo, 1.0, -1.0).astype(F32)

    def twice(k, j):
        w = w_ref[k, j]
        return jnp.concatenate([w, w], axis=0)

    def mix(k, carry):
        for j in range(J):
            rows = pl.ds(j * M + k, ND, stride=128)
            v = v_ref[rows, :]
            lhs = jnp.concatenate([jnp.where(lo, v, 0.0), jnp.where(lo, 0.0, v)], axis=0)
            res = dot(lhs.astype(BF16), twice(k, j))
            m_ref[rows, :] = res[:ND] - swap(res[ND:]) * sign
        return carry

    lax.fori_loop(0, M, mix, 0, unroll=2)
    narrow_dp(1)
    exchange_dp(1)
    arrived_dp(1)
    x_inverse(1, 1)
    exchange_space(1)
    cot_copy.wait()
    arrived_space(1)
    y_inverse(1)

    def middle(q, carry):
        cells = pl.ds(pl.multiple_of(q * 256, 256), 256)
        pre = z_inverse(zih, q) + dot(mix_in[...], x_ref[:, cells]) + bias_ref[...]
        cdf = 0.5 * (1.0 + lax.erf(pre * math.sqrt(0.5)))
        out_ref[:, cells] = (pre * cdf).astype(BF16)
        pdf = jnp.exp(-0.5 * pre * pre) * (1.0 / math.sqrt(2.0 * math.pi))
        gp = (cot_ref[:, cells].astype(F32) * (cdf + pre * pdf)).astype(BF16)
        gp_ref[:, cells] = gp
        return carry

    lax.fori_loop(0, BLOCKS, middle, 0)
    out_copy = pltpu.make_async_copy(out_ref, out_hbm, sem_local.at[2])
    out_copy.start()

    def second(q, carry):
        cells = pl.ds(pl.multiple_of(q * 256, 256), 256)
        z_forward(gp_ref[:, cells], zfh, q)
        return carry

    lax.fori_loop(0, BLOCKS, second, 0, unroll=2)
    y_forward(2)
    exchange_space(2)
    arrived_space(2)
    x_forward(2, 2)
    exchange_dp(2)
    arrived_dp(2)
    widen_dp(2, u_ref)

    def mix_grad(k, carry):
        for j in range(J):
            rows = pl.ds(j * M + k, ND, stride=128)
            g = u_ref[rows, :]
            lhs = jnp.concatenate([g, swap(g) * sign], axis=0)
            res = dot(lhs.astype(BF16), twice(k, j), NT)
            m_ref[rows, :] = jnp.where(lo, res[:ND], res[ND:])
        return carry

    lax.fori_loop(0, M, mix_grad, 0, unroll=2)
    narrow_dp(3)
    exchange_dp(3)

    def weight_grad(k, carry):
        for j in range(J):
            rows = pl.ds(j * M + k, ND, stride=128)
            v = v_ref[rows, :]
            g = u_ref[rows, :]
            lhs = jnp.concatenate([v, swap(v)], axis=0).astype(BF16)
            rhs = jnp.concatenate([g, swap(g) * sign], axis=0).astype(BF16)
            gw_ref[k, j] = dot(lhs[:, :64], rhs, TN)
        return carry

    lax.fori_loop(0, M, weight_grad, 0)
    gw_copy = pltpu.make_async_copy(gw_ref, gw_hbm, sem_local.at[3])
    gw_copy.start()

    arrived_dp(3)
    x_inverse(3, 3)
    exchange_space(3)
    arrived_space(3)
    y_inverse(3)

    def last(q, carry):
        cells = pl.ds(pl.multiple_of(q * 256, 256), 256)
        gin_ref[:, cells] = (z_inverse(zi, q) + dot(mix_back[...], gp_ref[:, cells])).astype(BF16)
        return carry

    lax.fori_loop(0, BLOCKS, last, 0)
    gin_copy = pltpu.make_async_copy(gin_ref, gin_hbm, sem_local.at[4])
    gin_copy.start()

    for n in range(4):
        sent = send_s.at[n, pl.ds(0, NS - 1)]
        pltpu.make_async_copy(sent, sent, sem_send_s.at[n]).wait()
        sent = send_d.at[n, pl.ds(0, ND - 1)]
        pltpu.make_async_copy(sent, sent, sem_send_d.at[n]).wait()
    out_copy.wait()
    gw_copy.wait()
    gin_copy.wait()


def local(fields, spec_weights, local_weight, bias, cotangent):
    x = fields.reshape(LANES, G * G)
    cot = cotangent.reshape(LANES, G * G)
    zero = jnp.zeros_like(local_weight)
    mix_back = jnp.block([[local_weight, zero], [zero, local_weight]])
    mix_in = mix_back.T
    bias2 = jnp.tile(bias, 2)[:, None]
    vmem = pl.BlockSpec(memory_space=pltpu.VMEM)
    hbm = pl.BlockSpec(memory_space=pl.ANY)
    consts = [jnp.asarray(t) for t in tables()]
    out, gin, gw = pl.pallas_call(
        kernel,
        out_shape=(
            jax.ShapeDtypeStruct(x.shape, BF16),
            jax.ShapeDtypeStruct(x.shape, BF16),
            jax.ShapeDtypeStruct(spec_weights.shape, F32),
        ),
        in_specs=[vmem] * 12 + [hbm] * 2,
        out_specs=(hbm, hbm, hbm),
        scratch_shapes=[
            pltpu.VMEM((M, J, 64, 128), BF16),
            pltpu.VMEM((LANES, G * G), BF16),
            pltpu.VMEM((LANES, G * G), BF16),
            pltpu.VMEM((LANES, G * G), BF16),
            pltpu.VMEM((LANES, G * G), BF16),
            pltpu.VMEM((M, J, 64, 128), F32),
            pltpu.VMEM((4096, LANES), F32),
            pltpu.VMEM((2048, LANES), F32),
            pltpu.VMEM((1024, LANES), F32),
            pltpu.VMEM((1024, LANES), F32),
            pltpu.VMEM((1024, LANES), F32),
            pltpu.VMEM((4, NS, J, 16, LANES), BF16),
            pltpu.VMEM((4, NS, J, 16, LANES), BF16),
            pltpu.VMEM((4, ND, J, M, LANES), BF16),
            pltpu.VMEM((4, ND, J, M, LANES), BF16),
            pltpu.SemaphoreType.DMA((4,)),
            pltpu.SemaphoreType.DMA((4,)),
            pltpu.SemaphoreType.DMA((4,)),
            pltpu.SemaphoreType.DMA((4,)),
            pltpu.SemaphoreType.DMA((5,)),
        ],
        compiler_params=pltpu.CompilerParams(
            collective_id=0, has_side_effects=True, vmem_limit_bytes=48 * 2**20
        ),
        cost_estimate=pl.CostEstimate(
            flops=2 * 10**9, bytes_accessed=12 * 2**20, transcendentals=2 * 10**6
        ),
    )(x, mix_in, mix_back, bias2, *consts, spec_weights, cot)
    shape = fields.shape
    return out.reshape(shape), gin.reshape(shape), gw


def solution(mesh):
    placed = (
        P("dp", "space", None, None),
        P(None, ("dp", "space"), None, None),
        P(),
        P(),
        P("dp", "space", None, None),
    )
    return jax.shard_map(
        local,
        mesh=mesh,
        in_specs=placed,
        out_specs=(
            P("dp", "space", None, None),
            P("dp", "space", None, None),
            P(None, ("dp", "space"), None, None),
        ),
        check_vma=False,
    )
```

profile of v0, /device:TPU:1, one launch (start us, length us, event | category | flops | bytes accessed | tf_op | source)
XLA Modules:
  0.0 125.4 jit_solution(9215159529457036170)
XLA Ops:
  0.6 0.7 tile.2
  1.3 0.1 broadcast_in_dim_tile.4.bias_ref
  1.4 0.9 fusion.2
  2.3 0.1 copy.16.mix_in
  2.4 0.0 copy-start
  2.4 1.2 copy-done
  3.7 0.0 copy-start.1
  3.7 1.2 copy-done.1
  4.9 0.0 copy-start.2
  4.9 0.9 copy-done.2
  5.8 0.0 copy-start.3
  5.8 0.9 copy-done.3
  6.7 0.0 copy-start.4
  6.7 0.9 copy-done.4
  7.6 0.0 copy-start.5
  7.6 0.9 copy-done.5
  8.5 0.0 copy-start.6
  8.5 0.8 copy-done.6
  9.3 0.0 copy-start.7
  9.3 0.8 copy-done.7
  10.0 0.0 copy-start.8
  10.0 0.8 copy-done.8
  10.8 0.0 copy-start.9
  10.8 0.7 copy-done.9
  11.5 109.0 %shard_map.148 = (bf16[128,4096]{1,0:T(8,128)(2,1)S(1)}, bf16[128,4096]{1,0:T(8,128)(2,1)S(1)}, f32[32,4,64,128]{3,2,1,0:T(8,128)}) custom-call(bf16[128,4096]{1,0:T(8,128)(2,1)S(1)} %bitcast.8, bf16[128,128]{1,0:T(8,128)(2,1)S(1)} %copy.16.mix_in, bf16[128,128]{1,0:T(8,128)(2,1)S(1)} %get-tuple-element.9.mix_back, ...), custom_call_target="tpu_custom_call" | custom-call | flops 2000000000 | bytes 12582912 | tf_op jit(solution)/shard_map/pallas_call | solution.py:398
  120.5 0.0 copy-start.10
  120.5 1.0 copy.21
  121.5 1.0 copy.22
  122.4 1.0 copy-done.10
  123.4 2.0 %copy.23 = f32[32,4,64,128]{3,2,1,0:T(8,128)} copy(f32[32,4,64,128]{3,2,1,0:T(8,128)S(1)} %copy-done.10) | data formatting | bytes 8388608
Async XLA Ops:
  2.4 1.2 copy-start
  3.7 1.2 copy-start.1
  4.9 0.9 copy-start.2
  5.8 0.9 copy-start.3
  6.7 0.9 copy-start.4
  7.6 0.9 copy-start.5
  8.5 0.8 copy-start.6
  9.3 0.8 copy-start.7
  10.0 0.8 copy-start.8
  10.8 0.7 copy-start.9
  120.5 2.9 %copy-start.10 = (f32[32,4,64,128]{3,2,1,0:T(8,128)S(1)}, f32[32,4,64,128]{3,2,1,0:T(8,128)}, u32[]{:S(2)}) copy-start(f32[32,4,64,128]{3,2,1,0:T(8,128)} %get-tuple-element.16) | copy-start | bytes 12582916
where the time goes:
time: 126 us; the launch traced here: 125 us
  Pallas kernels  109 us (87%)
  local copies, waits for them, and re-layouts  14.9 us (12%)
    pallas_call x1, Pallas kernels, local(): pl.pallas_call(kernel, out_shape=(jax.ShapeDtypeStruct(x.shape, BF16), ja...  109 us
    unnamed x25, local copies, waits for them, and re-layouts  14 us

commit v1 on v0

v1 whole, which is shorter than its diff:
```python
import functools
import math

import jax
import jax.numpy as jnp
import ml_dtypes
import numpy as np
from jax import lax
from jax.experimental import pallas as pl
from jax.experimental.pallas import tpu as pltpu
from jax.sharding import PartitionSpec as P

MESH = pl.DeviceIdType.MESH
BF16 = jnp.bfloat16
F32 = jnp.float32

G = 64
M = 32
NS = 32
ND = 8
J = 4
LANES = 128
BLOCKS = 16

NT = (((1,), (1,)), ((), ()))
TN = (((0,), (0,)), ((), ()))


def tables():
    step = 2.0 * math.pi / G
    cell = np.arange(G)
    freq_z = np.arange(M)
    signed = np.where(np.arange(M) < M // 2, np.arange(M), G - M + np.arange(M))
    halves = np.where(freq_z == 0, 1.0, 2.0)
    angle = (freq_z[:, None] * cell[None, :] % G) * step
    z_rows = np.concatenate([np.cos(angle), -np.sin(angle)]) / 8
    z_rows_half = z_rows * np.tile(halves, 2)[:, None]
    four = np.eye(4)
    z_forward = np.kron(four, z_rows)
    z_forward_half = np.kron(four, z_rows_half)
    inv = np.stack([np.cos(angle), -np.sin(angle)], axis=1).reshape(2 * M, G) / 8
    inv_half = inv * np.repeat(halves, 2)[:, None]
    z_inverse = np.kron(four, inv)
    z_inverse_half = np.kron(four, inv_half)
    iy = np.arange(ND)[None, :] * 4 + np.arange(4)[:, None]
    ang_y = (signed[iy][:, :, None] * cell % G) * step
    c, s = np.cos(ang_y) / 8, np.sin(ang_y) / 8
    y_forward = np.stack([np.stack([c, s], -1), np.stack([-s, c], -1)], 1).reshape(64, 128)
    ct, st = c.transpose(2, 0, 1), s.transpose(2, 0, 1)
    y_inverse = np.stack([np.stack([ct, -st], 2), np.stack([st, ct], 2)], 0).reshape(128, 64)
    xs = 2 * np.arange(NS)[None, :] + np.arange(2)[:, None]
    ang_x = (signed[None, :, None] * xs[:, None, :] % G) * step
    c, s = np.cos(ang_x) / 8, np.sin(ang_x) / 8
    x_forward = np.stack([np.stack([c, s], 2), np.stack([-s, c], 2)], 1)
    x_forward = x_forward.reshape(128, 64)
    x_inverse = np.stack([c.transpose(0, 2, 1), s.transpose(0, 2, 1)]).reshape(128, M)
    return [
        t.astype(np.float32).astype(ml_dtypes.bfloat16)
        for t in (
            z_forward, z_forward_half, z_inverse, z_inverse_half,
            y_forward, y_inverse, x_forward, x_inverse,
        )
    ]


def dot(a, b, dims=(((1,), (0,)), ((), ()))):
    return lax.dot_general(a, b, dims, preferred_element_type=F32)


def kernel(
    x_hbm, weight_hbm, bias_hbm, z_hbm, small_hbm, w_hbm, cot_hbm,
    out_hbm, gin_hbm, gw_hbm,
    x_ref, weight_ref, bias_ref, z_ref, small_ref, mix_ref,
    w_ref, cot_ref, out_ref, gp_ref, gin_ref, gw_ref,
    a_ref, e_ref, f_ref, v_ref, u_ref, m_ref,
    send_s, recv_s, send_d, recv_d,
    sem_send_s, sem_recv_s, sem_send_d, sem_recv_d, sem_local, sem_x,
):
    d = lax.axis_index("dp")
    s = lax.axis_index("space")

    def fetch(src, dst, sem):
        copy = pltpu.make_async_copy(src, dst, sem)
        copy.start()
        return copy

    quarter = G * G // 4
    z_copy = fetch(z_hbm, z_ref, sem_local.at[0])
    x_copies = [
        fetch(
            x_hbm.at[:, pl.ds(i * quarter, quarter)],
            x_ref.at[:, pl.ds(i * quarter, quarter)],
            sem_x.at[i],
        )
        for i in range(4)
    ]
    small_copy = fetch(small_hbm, small_ref, sem_local.at[1])
    weight_copy = fetch(weight_hbm, weight_ref, sem_local.at[2])
    bias_copy = fetch(bias_hbm, bias_ref, sem_local.at[3])
    w_copy = fetch(w_hbm, w_ref, sem_local.at[4])
    cot_copy = fetch(cot_hbm, cot_ref, sem_local.at[5])

    barrier = pltpu.get_barrier_semaphore()

    def greet_space(i, carry):
        pl.semaphore_signal(barrier, inc=1, device_id=(d, lax.rem(s + i, NS)), device_id_type=MESH)
        return carry

    def greet_dp(i, carry):
        pl.semaphore_signal(barrier, inc=1, device_id=(lax.rem(d + i, ND), s), device_id_type=MESH)
        return carry

    lax.fori_loop(1, NS, greet_space, 0)
    lax.fori_loop(1, ND, greet_dp, 0)

    lo = lax.broadcasted_iota(jnp.int32, (1, LANES), 1) < 64
    sign = jnp.where(lo, 1.0, -1.0).astype(F32)

    def swap(v):
        return pltpu.roll(v, 64, 1)

    def exchange_space(n, c):
        src, dst = send_s.at[n, c], recv_s.at[n, c]

        def go(i, carry):
            t = lax.rem(s + i, NS)
            pltpu.make_async_remote_copy(
                src_ref=src.at[t], dst_ref=dst.at[s],
                send_sem=sem_send_s.at[n, c], recv_sem=sem_recv_s.at[n, c],
                device_id=(d, t), device_id_type=MESH,
            ).start()
            return carry

        lax.fori_loop(1, NS, go, 0)
        pltpu.make_async_copy(src.at[s], dst.at[s], sem_recv_s.at[n, c]).start()

    def exchange_dp(n, c):
        src, dst = send_d.at[n, c], recv_d.at[n, c]

        def go(i, carry):
            t = lax.rem(d + i, ND)
            pltpu.make_async_remote_copy(
                src_ref=src.at[t], dst_ref=dst.at[d],
                send_sem=sem_send_d.at[n, c], recv_sem=sem_recv_d.at[n, c],
                device_id=(t, s), device_id_type=MESH,
            ).start()
            return carry

        lax.fori_loop(1, ND, go, 0)
        pltpu.make_async_copy(src.at[d], dst.at[d], sem_recv_d.at[n, c]).start()

    def arrived_space(n, c):
        pltpu.make_async_copy(recv_s.at[n, c], recv_s.at[n, c], sem_recv_s.at[n, c]).wait()

    def arrived_dp(n, c):
        pltpu.make_async_copy(recv_d.at[n, c], recv_d.at[n, c], sem_recv_d.at[n, c]).wait()

    def chunks(step):
        def go(c, carry):
            step(c)
            return carry

        lax.fori_loop(0, J, go, 0)

    def z_forward(block, table, q, to):
        to[pl.ds(pl.multiple_of(q * 256, 256), 256), :] = dot(z_ref[table], block, NT)

    def y_forward(n, c, source):
        table = small_ref[0, :64, :]
        for pair in range(4):
            parts = [
                source[pl.ds((pair * 2 + e) * 4 + c, 128, stride=M), :].astype(BF16)
                for e in range(2)
            ]
            res = dot(table, jnp.concatenate(parts, axis=1)).astype(BF16)
            for e in range(2):
                for iyl in range(4):
                    send_s[n, c, iyl * 8 + pair * 2 + e] = res[
                        iyl * 16 : iyl * 16 + 16, e * 128 : e * 128 + 128
                    ]

    def x_forward(n_space, n_dp, c):
        f_ref[...] = recv_s[n_space, c].reshape(NS * 16, LANES).astype(F32)
        table = small_ref[2, :, :64]
        for pair in range(4):
            parts = []
            for e in range(2):
                row = pair * 2 + e
                parts.append(
                    jnp.concatenate(
                        [
                            f_ref[pl.ds(row, NS, stride=16), :],
                            f_ref[pl.ds(row + 8, NS, stride=16), :],
                        ],
                        axis=0,
                    ).astype(BF16)
                )
            res = dot(table, jnp.concatenate(parts, axis=1))
            for e in range(2):
                p00, p01, p10, p11 = (
                    res[b * 32 : b * 32 + 32, e * 128 : e * 128 + 128] for b in range(4)
                )
                both = jnp.where(lo, p00, p11) + swap(jnp.where(lo, p01, p10))
                send_d[n_dp, c, pair * 2 + e] = both.astype(BF16)

    def widen_dp(n, c, to):
        to[c] = recv_d[n, c].reshape(ND * M, LANES).astype(F32)

    def narrow_dp(n, c):
        send_d[n, c] = m_ref[...].astype(BF16).reshape(ND, M, LANES)

    def x_inverse(n_dp, n_space, c):
        table = small_ref[3, :, :M]
        for pair in range(4):
            rhs = jnp.concatenate(
                [recv_d[n_dp, c, pair * 2], recv_d[n_dp, c, pair * 2 + 1]], axis=1
            )
            res = dot(table, rhs)
            for e in range(2):
                c0, c1, s0, s1 = (
                    res[b * 32 : b * 32 + 32, e * 128 : e * 128 + 128] for b in range(4)
                )
                row = pair * 2 + e
                f_ref[pl.ds(row, NS, stride=16), :] = jnp.where(lo, c0, -s1) + swap(
                    jnp.where(lo, c1, -s0)
                )
                f_ref[pl.ds(row + 8, NS, stride=16), :] = jnp.where(lo, s0, c1) + swap(
                    jnp.where(lo, s1, c0)
                )
        send_s[n_space, c] = f_ref[...].astype(BF16).reshape(NS, 16, LANES)

    def y_inverse(n, c):
        table = small_ref[1, :, :64]
        for pair in range(4):
            parts = [
                jnp.concatenate(
                    [recv_s[n, c, iyl * 8 + pair * 2 + e] for iyl in range(4)], axis=0
                )
                for e in range(2)
            ]
            res = dot(table, jnp.concatenate(parts, axis=1))
            for e in range(2):
                iz = (pair * 2 + e) * 4 + c
                a_ref[pl.ds(pl.multiple_of(iz * 128, 128), 128), :] = res[
                    :, e * 128 : e * 128 + 128
                ]

    def z_inverse(table, q):
        rows = [a_ref[pl.ds(q * 4 + yl, 64, stride=64), :] for yl in range(4)]
        return dot(jnp.concatenate(rows, axis=0).astype(BF16), z_ref[table], TN)

    z_copy.wait()
    for i in range(4):
        x_copies[i].wait()
        for q in range(4 * i, 4 * i + 4):
            z_forward(x_ref[:, q * 256 : q * 256 + 256], 0, q, e_ref)
    small_copy.wait()
    weight_copy.wait()
    bias_copy.wait()

    weight = weight_ref[...].astype(F32)
    zero = jnp.zeros((64, 64), F32)
    both = jnp.concatenate(
        [jnp.concatenate([weight, zero], axis=1), jnp.concatenate([zero, weight], axis=1)], axis=0
    )
    mix_ref[0] = both.T.astype(BF16)
    mix_ref[1] = both.astype(BF16)
    diagonal = lax.broadcasted_iota(jnp.int32, (64, 64), 0) == lax.broadcasted_iota(
        jnp.int32, (64, 64), 1
    )
    column = jnp.sum(jnp.where(diagonal, bias_ref[...], 0.0), axis=1, keepdims=True)
    bias = jnp.concatenate([column, column], axis=0)

    pl.semaphore_wait(barrier, NS + ND - 2)

    def out_space(n):
        def step(c):
            y_forward(n, c, e_ref)
            exchange_space(n, c)

        chunks(step)

    def out_dp(n):
        def step(c):
            arrived_space(n, c)
            x_forward(n, n, c)
            exchange_dp(n, c)

        chunks(step)

    def back_space(n):
        def step(c):
            arrived_dp(n, c)
            x_inverse(n, n, c)
            exchange_space(n, c)

        chunks(step)

    def back_grid(n):
        def step(c):
            arrived_space(n, c)
            y_inverse(n, c)

        chunks(step)

    out_space(0)
    out_dp(0)

    w_copy.wait()

    def twice(k, j):
        w = w_ref[k, j]
        return jnp.concatenate([w, w], axis=0)

    def mix(j):
        arrived_dp(0, j)
        widen_dp(0, j, v_ref)

        def go(k, carry):
            rows = pl.ds(k, ND, stride=M)
            v = v_ref[j, rows, :]
            lhs = jnp.concatenate([jnp.where(lo, v, 0.0), jnp.where(lo, 0.0, v)], axis=0)
            res = dot(lhs.astype(BF16), twice(k, j))
            m_ref[rows, :] = res[:ND] - swap(res[ND:]) * sign
            return carry

        lax.fori_loop(0, M, go, 0, unroll=8)
        narrow_dp(1, j)
        exchange_dp(1, j)

    chunks(mix)
    back_space(1)
    cot_copy.wait()
    back_grid(1)

    def middle(q, carry):
        cells = pl.ds(pl.multiple_of(q * 256, 256), 256)
        pre = z_inverse(3, q) + dot(mix_ref[0], x_ref[:, cells]) + bias
        cdf = 0.5 * (1.0 + lax.erf(pre * math.sqrt(0.5)))
        out_ref[:, cells] = (pre * cdf).astype(BF16)
        pdf = jnp.exp(-0.5 * pre * pre) * (1.0 / math.sqrt(2.0 * math.pi))
        gp = (cot_ref[:, cells].astype(F32) * (cdf + pre * pdf)).astype(BF16)
        gp_ref[:, cells] = gp
        z_forward(gp, 1, q, e_ref)
        return carry

    lax.fori_loop(0, BLOCKS, middle, 0, unroll=2)
    out_copy = fetch(out_ref, out_hbm, sem_local.at[6])

    out_space(2)
    out_dp(2)

    def mix_grad(j):
        arrived_dp(2, j)
        widen_dp(2, j, u_ref)

        def go(k, carry):
            rows = pl.ds(k, ND, stride=M)
            g = u_ref[j, rows, :]
            lhs = jnp.concatenate([g, swap(g) * sign], axis=0)
            res = dot(lhs.astype(BF16), twice(k, j), NT)
            m_ref[rows, :] = jnp.where(lo, res[:ND], res[ND:])
            return carry

        lax.fori_loop(0, M, go, 0, unroll=8)
        narrow_dp(3, j)
        exchange_dp(3, j)

    chunks(mix_grad)

    def weight_grad(j):
        def go(k, carry):
            rows = pl.ds(k, ND, stride=M)
            v = v_ref[j, rows, :]
            g = u_ref[j, rows, :]
            lhs = jnp.concatenate([v, swap(v)], axis=0).astype(BF16)
            rhs = jnp.concatenate([g, swap(g) * sign], axis=0).astype(BF16)
            gw_ref[k, j] = dot(lhs[:, :64], rhs, TN)
            return carry

        lax.fori_loop(0, M, go, 0, unroll=8)

    def back_space_grad(c):
        arrived_dp(3, c)
        x_inverse(3, 3, c)
        exchange_space(3, c)
        weight_grad(c)

    chunks(back_space_grad)
    gw_copy = fetch(gw_ref, gw_hbm, sem_local.at[7])
    back_grid(3)

    def last(q, carry):
        cells = pl.ds(pl.multiple_of(q * 256, 256), 256)
        gin_ref[:, cells] = (z_inverse(2, q) + dot(mix_ref[1], gp_ref[:, cells])).astype(BF16)
        return carry

    lax.fori_loop(0, BLOCKS, last, 0, unroll=2)
    gin_copy = fetch(gin_ref, gin_hbm, sem_local.at[8])

    for n in range(4):

        def sent(c, n=n):
            part = send_s.at[n, c, pl.ds(0, NS - 1)]
            pltpu.make_async_copy(part, part, sem_send_s.at[n, c]).wait()
            part = send_d.at[n, c, pl.ds(0, ND - 1)]
            pltpu.make_async_copy(part, part, sem_send_d.at[n, c]).wait()

        chunks(sent)
    out_copy.wait()
    gw_copy.wait()
    gin_copy.wait()


def local(fields, spec_weights, local_weight, bias, cotangent):
    x = fields.reshape(LANES, G * G)
    cot = cotangent.reshape(LANES, G * G)
    made = tables()
    z_tables = jnp.asarray(np.stack(made[:4]))
    small = np.zeros((4, 128, 128), ml_dtypes.bfloat16)
    for i, t in enumerate(made[4:]):
        small[i, : t.shape[0], : t.shape[1]] = t
    hbm = pl.BlockSpec(memory_space=pltpu.HBM)
    out, gin, gw = pl.pallas_call(
        kernel,
        out_shape=(
            jax.ShapeDtypeStruct(x.shape, BF16),
            jax.ShapeDtypeStruct(x.shape, BF16),
            jax.ShapeDtypeStruct(spec_weights.shape, F32),
        ),
        in_specs=[hbm] * 7,
        out_specs=(hbm, hbm, hbm),
        scratch_shapes=[
            pltpu.VMEM((LANES, G * G), BF16),
            pltpu.VMEM((64, 64), BF16),
            pltpu.VMEM((1, 64), F32),
            pltpu.VMEM((4, 256, 256), BF16),
            pltpu.VMEM((4, 128, 128), BF16),
            pltpu.VMEM((2, 128, 128), BF16),
            pltpu.VMEM((M, J, 64, 128), BF16),
            pltpu.VMEM((LANES, G * G), BF16),
            pltpu.VMEM((LANES, G * G), BF16),
            pltpu.VMEM((LANES, G * G), BF16),
            pltpu.VMEM((LANES, G * G), BF16),
            pltpu.VMEM((M, J, 64, 128), F32),
            pltpu.VMEM((4096, LANES), F32),
            pltpu.VMEM((4096, LANES), F32),
            pltpu.VMEM((NS * 16, LANES), F32),
            pltpu.VMEM((J, ND * M, LANES), F32),
            pltpu.VMEM((J, ND * M, LANES), F32),
            pltpu.VMEM((ND * M, LANES), F32),
            pltpu.VMEM((4, J, NS, 16, LANES), BF16),
            pltpu.VMEM((4, J, NS, 16, LANES), BF16),
            pltpu.VMEM((4, J, ND, M, LANES), BF16),
            pltpu.VMEM((4, J, ND, M, LANES), BF16),
            pltpu.SemaphoreType.DMA((4, J)),
            pltpu.SemaphoreType.DMA((4, J)),
            pltpu.SemaphoreType.DMA((4, J)),
            pltpu.SemaphoreType.DMA((4, J)),
            pltpu.SemaphoreType.DMA((9,)),
            pltpu.SemaphoreType.DMA((4,)),
        ],
        compiler_params=pltpu.CompilerParams(
            collective_id=0, has_side_effects=True, vmem_limit_bytes=63 * 2**20
        ),
        cost_estimate=pl.CostEstimate(
            flops=2 * 10**9, bytes_accessed=12 * 2**20, transcendentals=2 * 10**6
        ),
    )(x, local_weight, bias.reshape(1, 64), z_tables, jnp.asarray(small), spec_weights, cot)
    shape = fields.shape
    return out.reshape(shape), gin.reshape(shape), gw


def solution(mesh):
    placed = (
        P("dp", "space", None, None),
        P(None, ("dp", "space"), None, None),
        P(),
        P(),
        P("dp", "space", None, None),
    )
    return jax.shard_map(
        local,
        mesh=mesh,
        in_specs=placed,
        out_specs=(
            P("dp", "space", None, None),
            P("dp", "space", None, None),
            P(None, ("dp", "space"), None, None),
        ),
        check_vma=False,
    )
```

time: 126 us -> 84.8 us (0.67)
  Pallas kernels: 109 us -> 77.3 us
  local copies, waits for them, and re-layouts: 14.9 us -> 6.74 us
    pallas_call x1, Pallas kernels: 109 us -> 77.3 us  [local(): pl.pallas_call(kernel, out_shape=(jax.ShapeDtypeStruct(x.shape, BF16), ja...]
    unnamed x25 -> x5, local copies, waits for them, and re-layouts: 14 us -> 6.74 us
where the time goes in v1:
time: 84.8 us; the launch traced here: 84.7 us
  Pallas kernels  77.3 us (91%)
  local copies, waits for them, and re-layouts  6.74 us (8%)
    pallas_call x1, Pallas kernels, local(): pl.pallas_call(kernel, out_shape=(jax.ShapeDtypeStruct(x.shape, BF16), ja...  77.3 us
    unnamed x5, local copies, waits for them, and re-layouts  6.74 us

profile of v1, /device:TPU:1, one launch (start us, length us, event | category | flops | bytes accessed | tf_op | source)
XLA Modules:
  0.0 84.7 jit_solution(15299661239505970096)
XLA Ops:
  0.6 77.3 %shard_map.94 = (bf16[128,4096]{1,0:T(8,128)(2,1)}, bf16[128,4096]{1,0:T(8,128)(2,1)}, f32[32,4,64,128]{3,2,1,0:T(8,128)}) custom-call(bf16[128,4096]{1,0:T(8,128)(2,1)} %bitcast.7, bf16[64,64]{1,0:T(8,128)(2,1)} %weight_hbm.1, f32[1,64]{1,0:T(1,128)} %bitcast.9, bf16[4,256,256]{2,1,0:T(8,128)(2,1)} %constant.4.clone.z_hbm, ...), custom_call_target="tpu_custom_call" | custom-call | flops 2000000000 | bytes 12582912 | tf_op jit(solution)/shard_map/pallas_call | solution.py:424
  78.0 0.0 copy-start
  78.0 2.4 %copy.13 = bf16[1,2,64,4096]{3,2,1,0:T(8,128)(2,1)} copy(bf16[1,2,64,4096]{3,2,1,0:T(8,128)(2,1)} %bitcast.6) | data formatting | bytes 2097152
  80.4 2.3 %copy.14 = bf16[1,2,64,4096]{3,2,1,0:T(8,128)(2,1)} copy(bf16[1,2,64,4096]{3,2,1,0:T(8,128)(2,1)} %bitcast.5) | data formatting | bytes 2097152
  82.7 0.0 copy-done
  82.7 2.0 %copy.15 = f32[32,4,64,128]{3,2,1,0:T(8,128)} copy(f32[32,4,64,128]{3,2,1,0:T(8,128)S(1)} %copy-done) | data formatting | bytes 8388608
Async XLA Ops:
  78.0 4.7 %copy-start = (f32[32,4,64,128]{3,2,1,0:T(8,128)S(1)}, f32[32,4,64,128]{3,2,1,0:T(8,128)}, u32[]{:S(2)}) copy-start(f32[32,4,64,128]{3,2,1,0:T(8,128)} %get-tuple-element.14) | copy-start | bytes 12582916

commit v2 on v1

v2 whole, which is shorter than its diff:
```python
import functools
import math

import jax
import jax.numpy as jnp
import ml_dtypes
import numpy as np
from jax import lax
from jax.experimental import pallas as pl
from jax.experimental.pallas import tpu as pltpu
from jax.sharding import PartitionSpec as P

MESH = pl.DeviceIdType.MESH
BF16 = jnp.bfloat16
F32 = jnp.float32

G = 64
M = 32
NS = 32
ND = 8
J = 4
LANES = 128
BLOCKS = 16

NT = (((1,), (1,)), ((), ()))
TN = (((0,), (0,)), ((), ()))


def tables():
    step = 2.0 * math.pi / G
    cell = np.arange(G)
    freq_z = np.arange(M)
    signed = np.where(np.arange(M) < M // 2, np.arange(M), G - M + np.arange(M))
    halves = np.where(freq_z == 0, 1.0, 2.0)
    angle = (freq_z[:, None] * cell[None, :] % G) * step
    z_rows = np.concatenate([np.cos(angle), -np.sin(angle)]) / 8
    z_rows_half = z_rows * np.tile(halves, 2)[:, None]
    four = np.eye(4)
    z_forward = np.kron(four, z_rows)
    z_forward_half = np.kron(four, z_rows_half)
    inv = np.stack([np.cos(angle), -np.sin(angle)], axis=1).reshape(2 * M, G) / 8
    inv_half = inv * np.repeat(halves, 2)[:, None]
    z_inverse, z_inverse_half = (
        np.kron(four, t).reshape(4, ND, J, 2, 256).transpose(2, 0, 1, 3, 4).reshape(J, 64, 256)
        for t in (inv, inv_half)
    )
    iy = np.arange(ND)[None, :] * 4 + np.arange(4)[:, None]
    ang_y = (signed[iy][:, :, None] * cell % G) * step
    c, s = np.cos(ang_y) / 8, np.sin(ang_y) / 8
    y_forward = np.stack([np.stack([c, s], -1), np.stack([-s, c], -1)], 1).reshape(64, 128)
    ct, st = c.transpose(2, 0, 1), s.transpose(2, 0, 1)
    y_inverse = np.stack([np.stack([ct, -st], 2), np.stack([st, ct], 2)], 0).reshape(128, 64)
    xs = 2 * np.arange(NS)[None, :] + np.arange(2)[:, None]
    ang_x = (signed[None, :, None] * xs[:, None, :] % G) * step
    c, s = np.cos(ang_x) / 8, np.sin(ang_x) / 8
    x_forward = np.stack([np.stack([c, s], 2), np.stack([-s, c], 2)], 1)
    x_forward = x_forward.reshape(128, 64)
    x_inverse = np.stack([c.transpose(0, 2, 1), s.transpose(0, 2, 1)]).reshape(128, M)
    return [
        t.astype(np.float32).astype(ml_dtypes.bfloat16)
        for t in (
            z_forward, z_forward_half, z_inverse, z_inverse_half,
            y_forward, y_inverse, x_forward, x_inverse,
        )
    ]


def dot(a, b, dims=(((1,), (0,)), ((), ()))):
    return lax.dot_general(a, b, dims, preferred_element_type=F32)


def farthest_first():
    def ring(i, n):
        return min(i, n - i)

    offsets = [(y, x, c) for y in range(4) for x in range(4) for c in range(2)][1:]
    offsets.sort(key=lambda o: -ring(o[0], 4) - ring(o[1], 4))
    return offsets, sorted(range(1, ND), key=lambda i: -ring(i, ND))


def kernel(
    x_hbm, weight_hbm, bias_hbm, zf_hbm, zi_hbm, small_hbm, w_hbm, cot_hbm,
    out_ref, gw_ref, acc_ref, a_ref, last_ref,
    x_ref, weight_ref, bias_ref, zf_ref, zi_ref, small_ref, mix_ref,
    w_ref, cot_ref, gp_ref,
    e_ref, f_ref, v_ref, u_ref, m_ref,
    send_s, recv_s, send_d, recv_d,
    sem_send_s, sem_recv_s, sem_send_d, sem_recv_d, sem_local, sem_x,
):
    d = lax.axis_index("dp")
    s = lax.axis_index("space")
    row_y, row_x, core = s // 8, lax.rem(s // 2, 4), lax.rem(s, 2)
    space_offsets, dp_offsets = farthest_first()

    def fetch(src, dst, sem):
        copy = pltpu.make_async_copy(src, dst, sem)
        copy.start()
        return copy

    quarter = G * G // 4
    zf_copy = fetch(zf_hbm, zf_ref, sem_local.at[0])
    x_copies = [
        fetch(
            x_hbm.at[:, pl.ds(i * quarter, quarter)],
            x_ref.at[:, pl.ds(i * quarter, quarter)],
            sem_x.at[i],
        )
        for i in range(4)
    ]
    small_copy = fetch(small_hbm, small_ref, sem_local.at[1])
    weight_copy = fetch(weight_hbm, weight_ref, sem_local.at[2])
    bias_copy = fetch(bias_hbm, bias_ref, sem_local.at[3])
    zi_copy = fetch(zi_hbm, zi_ref, sem_local.at[4])
    w_copy = fetch(w_hbm, w_ref, sem_local.at[5])
    cot_copy = fetch(cot_hbm, cot_ref, sem_local.at[6])

    barrier = pltpu.get_barrier_semaphore()

    def greet_space(i, carry):
        pl.semaphore_signal(barrier, inc=1, device_id=(d, lax.rem(s + i, NS)), device_id_type=MESH)
        return carry

    def greet_dp(i, carry):
        pl.semaphore_signal(barrier, inc=1, device_id=(lax.rem(d + i, ND), s), device_id_type=MESH)
        return carry

    lax.fori_loop(1, ND, greet_dp, 0)
    lax.fori_loop(1, NS, greet_space, 0)

    lo = lax.broadcasted_iota(jnp.int32, (1, LANES), 1) < 64
    sign = jnp.where(lo, 1.0, -1.0).astype(F32)

    def swap(v):
        return pltpu.roll(v, 64, 1)

    def exchange_space(n, c):
        src, dst = send_s.at[n, c], recv_s.at[n, c]
        for oy, ox, oc in space_offsets:
            t = lax.rem(row_y + oy, 4) * 8 + lax.rem(row_x + ox, 4) * 2 + lax.rem(core + oc, 2)
            pltpu.make_async_remote_copy(
                src_ref=src.at[t], dst_ref=dst.at[s],
                send_sem=sem_send_s.at[n, c], recv_sem=sem_recv_s.at[n, c],
                device_id=(d, t), device_id_type=MESH,
            ).start()
        pltpu.make_async_copy(src.at[s], dst.at[s], sem_recv_s.at[n, c]).start()

    def exchange_dp(n, g):
        src, dst = send_d.at[n, g], recv_d.at[n, g]
        for offset in dp_offsets:
            t = lax.rem(d + offset, ND)
            pltpu.make_async_remote_copy(
                src_ref=src.at[t], dst_ref=dst.at[d],
                send_sem=sem_send_d.at[n, g], recv_sem=sem_recv_d.at[n, g],
                device_id=(t, s), device_id_type=MESH,
            ).start()
        pltpu.make_async_copy(src.at[d], dst.at[d], sem_recv_d.at[n, g]).start()

    def arrived_space(n, c):
        pltpu.make_async_copy(recv_s.at[n, c], recv_s.at[n, c], sem_recv_s.at[n, c]).wait()

    def arrived_dp(n, g):
        pltpu.make_async_copy(recv_d.at[n, g], recv_d.at[n, g], sem_recv_d.at[n, g]).wait()

    def chunks(step, first=0, end=J):
        def go(c, carry):
            step(c)
            return carry

        lax.fori_loop(first, end, go, 0)

    def z_forward(block, table, q):
        e_ref[pl.ds(pl.multiple_of(q * 256, 256), 256), :] = dot(zf_ref[table], block, NT)

    def y_forward(n, c):
        table = small_ref[0, :64, :]
        for pair in range(4):
            parts = [
                e_ref[pl.ds((pair * 2 + e) * 4 + c, 128, stride=M), :].astype(BF16)
                for e in range(2)
            ]
            res = dot(table, jnp.concatenate(parts, axis=1)).astype(BF16)
            for e in range(2):
                for iyl in range(4):
                    send_s[n, c, iyl * 8 + pair * 2 + e] = res[
                        iyl * 16 : iyl * 16 + 16, e * 128 : e * 128 + 128
                    ]

    def x_forward(n_space, n_dp, c):
        f_ref[...] = recv_s[n_space, c].reshape(NS * 16, LANES).astype(F32)
        table = small_ref[2, :, :64]
        for pair in range(4):
            parts = []
            for e in range(2):
                row = pair * 2 + e
                parts.append(
                    jnp.concatenate(
                        [
                            f_ref[pl.ds(row, NS, stride=16), :],
                            f_ref[pl.ds(row + 8, NS, stride=16), :],
                        ],
                        axis=0,
                    ).astype(BF16)
                )
            res = dot(table, jnp.concatenate(parts, axis=1))
            for e in range(2):
                p00, p01, p10, p11 = (
                    res[b * 32 : b * 32 + 32, e * 128 : e * 128 + 128] for b in range(4)
                )
                both = jnp.where(lo, p00, p11) + swap(jnp.where(lo, p01, p10))
                both = both.astype(BF16)
                for h in range(2):
                    send_d[n_dp, c * 2 + h, pair * 2 + e] = both[h * 16 : h * 16 + 16]

    def widen_dp(n, g, to):
        to[g] = recv_d[n, g].reshape(ND * 16, LANES).astype(F32)

    def narrow_dp(n, g):
        send_d[n, g] = m_ref[...].astype(BF16).reshape(ND, 16, LANES)

    def x_inverse(n_dp, n_space, c):
        table = small_ref[3, :, :M]
        for pair in range(4):
            rhs = jnp.concatenate(
                [
                    jnp.concatenate(
                        [recv_d[n_dp, c * 2 + h, pair * 2 + e] for h in range(2)], axis=0
                    )
                    for e in range(2)
                ],
                axis=1,
            )
            res = dot(table, rhs)
            for e in range(2):
                c0, c1, s0, s1 = (
                    res[b * 32 : b * 32 + 32, e * 128 : e * 128 + 128] for b in range(4)
                )
                row = pair * 2 + e
                f_ref[pl.ds(row, NS, stride=16), :] = jnp.where(lo, c0, -s1) + swap(
                    jnp.where(lo, c1, -s0)
                )
                f_ref[pl.ds(row + 8, NS, stride=16), :] = jnp.where(lo, s0, c1) + swap(
                    jnp.where(lo, s1, c0)
                )
        send_s[n_space, c] = f_ref[...].astype(BF16).reshape(NS, 16, LANES)

    def y_inverse(n, c):
        table = small_ref[1, :, :64]
        for pair in range(4):
            parts = [
                jnp.concatenate(
                    [recv_s[n, c, iyl * 8 + pair * 2 + e] for iyl in range(4)], axis=0
                )
                for e in range(2)
            ]
            res = dot(table, jnp.concatenate(parts, axis=1))
            for e in range(2):
                izh = pair * 2 + e
                a_ref[izh * 128 : izh * 128 + 128, :] = res[:, e * 128 : e * 128 + 128]

    def cells(q):
        return pl.ds(pl.multiple_of(q * 256, 256), 256)

    zf_copy.wait()
    for i in range(4):
        x_copies[i].wait()
        for q in range(4 * i, 4 * i + 4):
            z_forward(x_ref[:, q * 256 : q * 256 + 256], 0, q)
    small_copy.wait()
    weight_copy.wait()
    bias_copy.wait()
    chunks(lambda c: y_forward(0, c))

    weight = weight_ref[...].astype(F32)
    zero = jnp.zeros((64, 64), F32)
    both = jnp.concatenate(
        [jnp.concatenate([weight, zero], axis=1), jnp.concatenate([zero, weight], axis=1)], axis=0
    )
    mix_ref[0] = both.T.astype(BF16)
    mix_ref[1] = both.astype(BF16)
    diagonal = lax.broadcasted_iota(jnp.int32, (64, 64), 0) == lax.broadcasted_iota(
        jnp.int32, (64, 64), 1
    )
    column = jnp.sum(jnp.where(diagonal, bias_ref[...], 0.0), axis=1, keepdims=True)
    bias = jnp.concatenate([column, column], axis=0)

    pl.semaphore_wait(barrier, NS + ND - 2)
    chunks(lambda c: exchange_space(0, c))

    def pointwise(q, carry):
        acc_ref[:, cells(q)] = dot(mix_ref[0], x_ref[:, cells(q)]) + bias
        return carry

    lax.fori_loop(0, BLOCKS, pointwise, 0, unroll=4)
    zi_copy.wait()
    last_ref[...] = zi_ref[0, J - 1]

    def out_dp(n):
        def step(c):
            arrived_space(n, c)
            x_forward(n, n, c)
            exchange_dp(n, c * 2)
            exchange_dp(n, c * 2 + 1)

        chunks(step)

    def back_space(n, c):
        arrived_dp(n, c * 2)
        arrived_dp(n, c * 2 + 1)
        x_inverse(n, n, c)
        exchange_space(n, c)

    def back_grid(n, table, c):
        arrived_space(n, c)
        y_inverse(n, c)

        def go(q, carry):
            acc_ref[:, cells(q)] += z_part(a_ref, zi_ref[table, c], q)
            return carry

        lax.fori_loop(0, BLOCKS, go, 0, unroll=4)

    out_dp(0)

    w_copy.wait()

    def twice(k, j):
        w = w_ref[k, j]
        return jnp.concatenate([w, w], axis=0)

    def mix(g):
        j, base = g // 2, lax.rem(g, 2) * 16
        arrived_dp(0, g)
        widen_dp(0, g, v_ref)

        def go(k, carry):
            rows = pl.ds(k, ND, stride=16)
            v = v_ref[g, rows, :]
            lhs = jnp.concatenate([jnp.where(lo, v, 0.0), jnp.where(lo, 0.0, v)], axis=0)
            res = dot(lhs.astype(BF16), twice(base + k, j))
            m_ref[rows, :] = res[:ND] - swap(res[ND:]) * sign
            return carry

        lax.fori_loop(0, 16, go, 0, unroll=16)
        narrow_dp(1, g)
        exchange_dp(1, g)

    chunks(mix, 0, 2 * J)
    chunks(lambda c: back_space(1, c))
    cot_copy.wait()
    chunks(lambda c: back_grid(1, 1, c), 0, J - 1)
    arrived_space(1, J - 1)
    y_inverse(1, J - 1)

    def middle(q, carry):
        pre = acc_ref[:, cells(q)] + z_part(a_ref, zi_ref[1, J - 1], q)
        cdf = 0.5 * (1.0 + lax.erf(pre * math.sqrt(0.5)))
        out_ref[:, cells(q)] = (pre * cdf).astype(BF16)
        pdf = jnp.exp(-0.5 * pre * pre) * (1.0 / math.sqrt(2.0 * math.pi))
        gp = (cot_ref[:, cells(q)].astype(F32) * (cdf + pre * pdf)).astype(BF16)
        gp_ref[:, cells(q)] = gp
        z_forward(gp, 1, q)
        return carry

    lax.fori_loop(0, BLOCKS, middle, 0, unroll=2)

    def out_space(c):
        y_forward(2, c)
        exchange_space(2, c)

    chunks(out_space)

    def pointwise_back(q, carry):
        acc_ref[:, cells(q)] = dot(mix_ref[1], gp_ref[:, cells(q)])
        return carry

    lax.fori_loop(0, BLOCKS, pointwise_back, 0, unroll=4)
    out_dp(2)

    def mix_grad(g):
        j, base = g // 2, lax.rem(g, 2) * 16
        arrived_dp(2, g)
        widen_dp(2, g, u_ref)

        def go(k, carry):
            rows = pl.ds(k, ND, stride=16)
            v = u_ref[g, rows, :]
            lhs = jnp.concatenate([v, swap(v) * sign], axis=0)
            res = dot(lhs.astype(BF16), twice(base + k, j), NT)
            m_ref[rows, :] = jnp.where(lo, res[:ND], res[ND:])
            return carry

        lax.fori_loop(0, 16, go, 0, unroll=16)
        narrow_dp(3, g)
        exchange_dp(3, g)

    chunks(mix_grad, 0, 2 * J)

    def weight_grad(g):
        j, base = g // 2, lax.rem(g, 2) * 16

        def go(k, carry):
            rows = pl.ds(k, ND, stride=16)
            v = v_ref[g, rows, :]
            grad = u_ref[g, rows, :]
            lhs = jnp.concatenate([v, swap(v)], axis=0).astype(BF16)
            rhs = jnp.concatenate([grad, swap(grad) * sign], axis=0).astype(BF16)
            gw_ref[base + k, j] = dot(lhs[:, :64], rhs, TN)
            return carry

        lax.fori_loop(0, 16, go, 0, unroll=8)

    def back_space_grad(c):
        back_space(3, c)
        weight_grad(c)

    chunks(back_space_grad, 0, 3)
    back_space(3, 3)

    def back_grid_grad(c):
        weight_grad(c * 2 + 3)
        back_grid(3, 0, c)
        weight_grad(c * 2 + 4)

    chunks(back_grid_grad, 0, 2)
    weight_grad(7)
    back_grid(3, 0, 2)
    arrived_space(3, J - 1)
    y_inverse(3, J - 1)

    for n in range(4):

        def sent_space(c, n=n):
            part = send_s.at[n, c, pl.ds(0, NS - 1)]
            pltpu.make_async_copy(part, part, sem_send_s.at[n, c]).wait()

        def sent_dp(g, n=n):
            part = send_d.at[n, g, pl.ds(0, ND - 1)]
            pltpu.make_async_copy(part, part, sem_send_d.at[n, g]).wait()

        chunks(sent_space)
        chunks(sent_dp, 0, 2 * J)


def z_part(a_ref, table, q):
    rows = [a_ref[pl.ds(q * 4 + yl, 16, stride=64), :] for yl in range(4)]
    return dot(jnp.concatenate(rows, axis=0).astype(BF16), table, TN)


def finish(
    out_ref, gw_ref, acc_ref, a_ref, last_ref,
    out_hbm, gin_hbm, gw_hbm,
    gin_ref, sem, sem_gin,
):
    copies = [
        pltpu.make_async_copy(gw_ref, gw_hbm, sem.at[0]),
        pltpu.make_async_copy(out_ref, out_hbm, sem.at[1]),
    ]
    for copy in copies:
        copy.start()
    quarter = G * G // 4
    for i in range(4):

        def last(q, carry):
            here = pl.ds(pl.multiple_of(q * 256, 256), 256)
            gin_ref[:, here] = (acc_ref[:, here] + z_part(a_ref, last_ref[...], q)).astype(BF16)
            return carry

        lax.fori_loop(4 * i, 4 * i + 4, last, 0, unroll=4)
        part = pl.ds(i * quarter, quarter)
        copy = pltpu.make_async_copy(gin_ref.at[:, part], gin_hbm.at[:, part], sem_gin.at[i])
        copy.start()
        copies.append(copy)
    for copy in copies:
        copy.wait()


def local(fields, spec_weights, local_weight, bias, cotangent):
    x = fields.reshape(LANES, G * G)
    cot = cotangent.reshape(LANES, G * G)
    made = tables()
    zf_tables = jnp.asarray(np.stack(made[0:2]))
    zi_tables = jnp.asarray(np.stack(made[2:4]))
    small = np.zeros((4, 128, 128), ml_dtypes.bfloat16)
    for i, t in enumerate(made[4:]):
        small[i, : t.shape[0], : t.shape[1]] = t
    hbm = pl.BlockSpec(memory_space=pltpu.HBM)
    vmem = pl.BlockSpec(memory_space=pltpu.VMEM)
    parts = pl.pallas_call(
        kernel,
        out_shape=(
            pltpu.VMEM(x.shape, BF16),
            pltpu.VMEM(spec_weights.shape, F32),
            pltpu.VMEM(x.shape, F32),
            pltpu.VMEM((1024, LANES), F32),
            pltpu.VMEM((64, 256), BF16),
        ),
        in_specs=[hbm] * 8,
        out_specs=(vmem,) * 5,
        scratch_shapes=[
            pltpu.VMEM((LANES, G * G), BF16),
            pltpu.VMEM((64, 64), BF16),
            pltpu.VMEM((1, 64), F32),
            pltpu.VMEM((2, 256, 256), BF16),
            pltpu.VMEM((2, J, 64, 256), BF16),
            pltpu.VMEM((4, 128, 128), BF16),
            pltpu.VMEM((2, 128, 128), BF16),
            pltpu.VMEM((M, J, 64, 128), BF16),
            pltpu.VMEM((LANES, G * G), BF16),
            pltpu.VMEM((LANES, G * G), BF16),
            pltpu.VMEM((4096, LANES), F32),
            pltpu.VMEM((NS * 16, LANES), F32),
            pltpu.VMEM((2 * J, ND * 16, LANES), F32),
            pltpu.VMEM((2 * J, ND * 16, LANES), F32),
            pltpu.VMEM((ND * 16, LANES), F32),
            pltpu.VMEM((4, J, NS, 16, LANES), BF16),
            pltpu.VMEM((4, J, NS, 16, LANES), BF16),
            pltpu.VMEM((4, 2 * J, ND, 16, LANES), BF16),
            pltpu.VMEM((4, 2 * J, ND, 16, LANES), BF16),
            pltpu.SemaphoreType.DMA((4, J)),
            pltpu.SemaphoreType.DMA((4, J)),
            pltpu.SemaphoreType.DMA((4, 2 * J)),
            pltpu.SemaphoreType.DMA((4, 2 * J)),
            pltpu.SemaphoreType.DMA((7,)),
            pltpu.SemaphoreType.DMA((4,)),
        ],
        compiler_params=pltpu.CompilerParams(
            collective_id=0, has_side_effects=True, vmem_limit_bytes=55 * 2**20
        ),
        cost_estimate=pl.CostEstimate(
            flops=2 * 10**9, bytes_accessed=12 * 2**20, transcendentals=2 * 10**6
        ),
    )(x, local_weight, bias.reshape(1, 64), zf_tables, zi_tables, jnp.asarray(small), spec_weights, cot)
    out, gin, gw = pl.pallas_call(
        finish,
        out_shape=(
            jax.ShapeDtypeStruct(x.shape, BF16),
            jax.ShapeDtypeStruct(x.shape, BF16),
            jax.ShapeDtypeStruct(spec_weights.shape, F32),
        ),
        in_specs=[vmem] * 5,
        out_specs=(hbm, hbm, hbm),
        scratch_shapes=[
            pltpu.VMEM(x.shape, BF16),
            pltpu.SemaphoreType.DMA((2,)),
            pltpu.SemaphoreType.DMA((4,)),
        ],
        compiler_params=pltpu.CompilerParams(vmem_limit_bytes=4 * 2**20),
    )(*parts)
    shape = fields.shape
    return out.reshape(shape), gin.reshape(shape), gw


def solution(mesh):
    placed = (
        P("dp", "space", None, None),
        P(None, ("dp", "space"), None, None),
        P(),
        P(),
        P("dp", "space", None, None),
    )
    return jax.shard_map(
        local,
        mesh=mesh,
        in_specs=placed,
        out_specs=(
            P("dp", "space", None, None),
            P("dp", "space", None, None),
            P(None, ("dp", "space"), None, None),
        ),
        check_vma=False,
    )
```

time: 84.8 us -> 75.7 us (0.89)
  local copies, waits for them, and re-layouts: 6.74 us -> 0 us
  Pallas kernels: 77.3 us -> 75 us
    unnamed x5 -> x0, local copies, waits for them, and re-layouts: 6.74 us -> none
    pallas_call x1 -> x2, Pallas kernels: 77.3 us -> 75 us  [the longest x1 72 us: local(): pl.pallas_call(kernel, out_shape=(pltpu.VMEM(x.shape, BF16), pltpu.VMEM(s...]
where the time goes in v2:
time: 75.7 us; the launch traced here: 75.6 us
  Pallas kernels  75 us (99%)
    pallas_call x1, Pallas kernels, local(): pl.pallas_call(kernel, out_shape=(pltpu.VMEM(x.shape, BF16), pltpu.VMEM(s...  72 us
    pallas_call x1, Pallas kernels, local(): pl.pallas_call(finish, out_shape=(jax.ShapeDtypeStruct(x.shape, BF16), ja...  2.91 us

profile of v2, /device:TPU:1, one launch (start us, length us, event | category | flops | bytes accessed | tf_op | source)
XLA Modules:
  0.0 75.6 jit_solution(2971919423524000347)
XLA Ops:
  0.6 72.0 %shard_map.103 = (bf16[128,4096]{1,0:T(8,128)(2,1)S(1)}, f32[32,4,64,128]{3,2,1,0:T(8,128)S(1)}, f32[128,4096]{1,0:T(8,128)S(1)}, f32[1024,128]{1,0:T(8,128)S(1)}, bf16[64,256]{1,0:T(8,128)(2,1)S(1)}) custom-call(bf16[128,4096]{1,0:T(8,128)(2,1)} %bitcast.5, bf16[64,64]{1,0:T(8,128)(2,1)} %weight_hbm.1, f32[1,64]{1,0:T(1,128)} %bitcast.9, ...), custom_call_target="tpu_custom_call" | custom-call | flops 2000000000 | bytes 12582912 | tf_op jit(solution)/shard_map/pallas_call | solution.py:488
  72.7 2.9 %shard_map.104 = (bf16[128,4096]{1,0:T(8,128)(2,1)}, bf16[128,4096]{1,0:T(8,128)(2,1)}, f32[32,4,64,128]{3,2,1,0:T(8,128)}) custom-call(bf16[128,4096]{1,0:T(8,128)(2,1)S(1)} %get-tuple-element.11.out_ref, f32[32,4,64,128]{3,2,1,0:T(8,128)S(1)} %get-tuple-element.12.gw_ref, f32[128,4096]{1,0:T(8,128)S(1)} %get-tuple-element.13.acc_ref, ...), custom_call_target="tpu_custom_call" | custom-call | tf_op jit(solution)/shard_map/pallas_call | solution.py:533

commit v3 on v2

--- a/solution.py
+++ b/solution.py
@@ -290,7 +290,7 @@
         acc_ref[:, cells(q)] = dot(mix_ref[0], x_ref[:, cells(q)]) + bias
         return carry
 
-    lax.fori_loop(0, BLOCKS, pointwise, 0, unroll=4)
+    lax.fori_loop(0, BLOCKS, pointwise, 0, unroll=16)
     zi_copy.wait()
     last_ref[...] = zi_ref[0, J - 1]
 
@@ -317,7 +317,7 @@
             acc_ref[:, cells(q)] += z_part(a_ref, zi_ref[table, c], q)
             return carry
 
-        lax.fori_loop(0, BLOCKS, go, 0, unroll=4)
+        lax.fori_loop(0, BLOCKS, go, 0, unroll=16)
 
     out_dp(0)
 
@@ -361,7 +361,7 @@
         z_forward(gp, 1, q)
         return carry
 
-    lax.fori_loop(0, BLOCKS, middle, 0, unroll=2)
+    lax.fori_loop(0, BLOCKS, middle, 0, unroll=16)
 
     def out_space(c):
         y_forward(2, c)
@@ -373,7 +373,7 @@
         acc_ref[:, cells(q)] = dot(mix_ref[1], gp_ref[:, cells(q)])
         return carry
 
-    lax.fori_loop(0, BLOCKS, pointwise_back, 0, unroll=4)
+    lax.fori_loop(0, BLOCKS, pointwise_back, 0, unroll=16)
     out_dp(2)
 
     def mix_grad(g):
@@ -407,7 +407,7 @@
             gw_ref[base + k, j] = dot(lhs[:, :64], rhs, TN)
             return carry
 
-        lax.fori_loop(0, 16, go, 0, unroll=8)
+        lax.fori_loop(0, 16, go, 0, unroll=16)
 
     def back_space_grad(c):
         back_space(3, c)

time: 75.7 us -> 70.7 us (0.934)
  Pallas kernels: 75 us -> 70 us
    pallas_call x1, Pallas kernels: 72 us -> 67.1 us  [local(): pl.pallas_call(kernel, out_shape=(pltpu.VMEM(x.shape, BF16), pltpu.VMEM(s...]
where the time goes in v3:
time: 70.7 us; the launch traced here: 70.6 us
  Pallas kernels  70 us (99%)
    pallas_call x1, Pallas kernels, local(): pl.pallas_call(kernel, out_shape=(pltpu.VMEM(x.shape, BF16), pltpu.VMEM(s...  67.1 us
    pallas_call x1, Pallas kernels, local(): pl.pallas_call(finish, out_shape=(jax.ShapeDtypeStruct(x.shape, BF16), ja...  2.91 us

profile of v3, /device:TPU:1, one launch (start us, length us, event | category | flops | bytes accessed | tf_op | source)
XLA Modules:
  0.0 70.6 jit_solution(14509796341768608167)
XLA Ops:
  0.6 67.1 %shard_map.103 = (bf16[128,4096]{1,0:T(8,128)(2,1)S(1)}, f32[32,4,64,128]{3,2,1,0:T(8,128)S(1)}, f32[128,4096]{1,0:T(8,128)S(1)}, f32[1024,128]{1,0:T(8,128)S(1)}, bf16[64,256]{1,0:T(8,128)(2,1)S(1)}) custom-call(bf16[128,4096]{1,0:T(8,128)(2,1)} %bitcast.5, bf16[64,64]{1,0:T(8,128)(2,1)} %weight_hbm.1, f32[1,64]{1,0:T(1,128)} %bitcast.9, ...), custom_call_target="tpu_custom_call" | custom-call | flops 2000000000 | bytes 12582912 | tf_op jit(solution)/shard_map/pallas_call | solution.py:488
  67.7 2.9 %shard_map.104 = (bf16[128,4096]{1,0:T(8,128)(2,1)}, bf16[128,4096]{1,0:T(8,128)(2,1)}, f32[32,4,64,128]{3,2,1,0:T(8,128)}) custom-call(bf16[128,4096]{1,0:T(8,128)(2,1)S(1)} %get-tuple-element.11.out_ref, f32[32,4,64,128]{3,2,1,0:T(8,128)S(1)} %get-tuple-element.12.gw_ref, f32[128,4096]{1,0:T(8,128)S(1)} %get-tuple-element.13.acc_ref, ...), custom_call_target="tpu_custom_call" | custom-call | tf_op jit(solution)/shard_map/pallas_call | solution.py:533

commit v4 on v3

--- a/solution.py
+++ b/solution.py
@@ -97,6 +97,19 @@
         copy.start()
         return copy
 
+    barrier = pltpu.get_barrier_semaphore()
+
+    def greet_space(i, carry):
+        pl.semaphore_signal(barrier, inc=1, device_id=(d, lax.rem(s + i, NS)), device_id_type=MESH)
+        return carry
+
+    def greet_dp(i, carry):
+        pl.semaphore_signal(barrier, inc=1, device_id=(lax.rem(d + i, ND), s), device_id_type=MESH)
+        return carry
+
+    lax.fori_loop(1, ND, greet_dp, 0)
+    lax.fori_loop(1, NS, greet_space, 0)
+
     quarter = G * G // 4
     zf_copy = fetch(zf_hbm, zf_ref, sem_local.at[0])
     x_copies = [
@@ -113,19 +126,6 @@
     zi_copy = fetch(zi_hbm, zi_ref, sem_local.at[4])
     w_copy = fetch(w_hbm, w_ref, sem_local.at[5])
     cot_copy = fetch(cot_hbm, cot_ref, sem_local.at[6])
-
-    barrier = pltpu.get_barrier_semaphore()
-
-    def greet_space(i, carry):
-        pl.semaphore_signal(barrier, inc=1, device_id=(d, lax.rem(s + i, NS)), device_id_type=MESH)
-        return carry
-
-    def greet_dp(i, carry):
-        pl.semaphore_signal(barrier, inc=1, device_id=(lax.rem(d + i, ND), s), device_id_type=MESH)
-        return carry
-
-    lax.fori_loop(1, ND, greet_dp, 0)
-    lax.fori_loop(1, NS, greet_space, 0)
 
     lo = lax.broadcasted_iota(jnp.int32, (1, LANES), 1) < 64
     sign = jnp.where(lo, 1.0, -1.0).astype(F32)
@@ -207,27 +207,19 @@
                     res[b * 32 : b * 32 + 32, e * 128 : e * 128 + 128] for b in range(4)
                 )
                 both = jnp.where(lo, p00, p11) + swap(jnp.where(lo, p01, p10))
-                both = both.astype(BF16)
-                for h in range(2):
-                    send_d[n_dp, c * 2 + h, pair * 2 + e] = both[h * 16 : h * 16 + 16]
+                send_d[n_dp, c, pair * 2 + e] = both.astype(BF16)
 
     def widen_dp(n, g, to):
-        to[g] = recv_d[n, g].reshape(ND * 16, LANES).astype(F32)
+        to[g] = recv_d[n, g].reshape(ND * M, LANES).astype(F32)
 
     def narrow_dp(n, g):
-        send_d[n, g] = m_ref[...].astype(BF16).reshape(ND, 16, LANES)
+        send_d[n, g] = m_ref[...].astype(BF16).reshape(ND, M, LANES)
 
     def x_inverse(n_dp, n_space, c):
         table = small_ref[3, :, :M]
         for pair in range(4):
             rhs = jnp.concatenate(
-                [
-                    jnp.concatenate(
-                        [recv_d[n_dp, c * 2 + h, pair * 2 + e] for h in range(2)], axis=0
-                    )
-                    for e in range(2)
-                ],
-                axis=1,
+                [recv_d[n_dp, c, pair * 2 + e] for e in range(2)], axis=1
             )
             res = dot(table, rhs)
             for e in range(2):
@@ -298,14 +290,12 @@
         def step(c):
             arrived_space(n, c)
             x_forward(n, n, c)
-            exchange_dp(n, c * 2)
-            exchange_dp(n, c * 2 + 1)
+            exchange_dp(n, c)
 
         chunks(step)
 
     def back_space(n, c):
-        arrived_dp(n, c * 2)
-        arrived_dp(n, c * 2 + 1)
+        arrived_dp(n, c)
         x_inverse(n, n, c)
         exchange_space(n, c)
 
@@ -328,40 +318,46 @@
         return jnp.concatenate([w, w], axis=0)
 
     def mix(g):
-        j, base = g // 2, lax.rem(g, 2) * 16
         arrived_dp(0, g)
         widen_dp(0, g, v_ref)
 
         def go(k, carry):
-            rows = pl.ds(k, ND, stride=16)
+            rows = pl.ds(k, ND, stride=M)
             v = v_ref[g, rows, :]
             lhs = jnp.concatenate([jnp.where(lo, v, 0.0), jnp.where(lo, 0.0, v)], axis=0)
-            res = dot(lhs.astype(BF16), twice(base + k, j))
+            res = dot(lhs.astype(BF16), twice(k, g))
             m_ref[rows, :] = res[:ND] - swap(res[ND:]) * sign
             return carry
 
-        lax.fori_loop(0, 16, go, 0, unroll=16)
+        lax.fori_loop(0, M, go, 0, unroll=16)
         narrow_dp(1, g)
         exchange_dp(1, g)
 
-    chunks(mix, 0, 2 * J)
+    chunks(mix)
     chunks(lambda c: back_space(1, c))
     cot_copy.wait()
     chunks(lambda c: back_grid(1, 1, c), 0, J - 1)
     arrived_space(1, J - 1)
     y_inverse(1, J - 1)
 
-    def middle(q, carry):
-        pre = acc_ref[:, cells(q)] + z_part(a_ref, zi_ref[1, J - 1], q)
-        cdf = 0.5 * (1.0 + lax.erf(pre * math.sqrt(0.5)))
-        out_ref[:, cells(q)] = (pre * cdf).astype(BF16)
-        pdf = jnp.exp(-0.5 * pre * pre) * (1.0 / math.sqrt(2.0 * math.pi))
-        gp = (cot_ref[:, cells(q)].astype(F32) * (cdf + pre * pdf)).astype(BF16)
-        gp_ref[:, cells(q)] = gp
-        z_forward(gp, 1, q)
+    def middle(pair, carry):
+        sums = z_part_pair(a_ref, zi_ref[1, J - 1], pair)
+        grads = []
+        for e in range(2):
+            q = pair * 2 + e
+            pre = acc_ref[:, cells(q)] + sums[e * 128 : e * 128 + 128]
+            cdf = 0.5 * (1.0 + lax.erf(pre * math.sqrt(0.5)))
+            out_ref[:, cells(q)] = (pre * cdf).astype(BF16)
+            pdf = jnp.exp(-0.5 * pre * pre) * (1.0 / math.sqrt(2.0 * math.pi))
+            gp = (cot_ref[:, cells(q)].astype(F32) * (cdf + pre * pdf)).astype(BF16)
+            gp_ref[:, cells(q)] = gp
+            grads.append(gp)
+        res = dot(zf_ref[1], jnp.concatenate(grads, axis=0), NT)
+        for e in range(2):
+            e_ref[cells(pair * 2 + e), :] = res[:, e * 128 : e * 128 + 128]
         return carry
 
-    lax.fori_loop(0, BLOCKS, middle, 0, unroll=16)
+    lax.fori_loop(0, BLOCKS // 2, middle, 0, unroll=BLOCKS // 2)
 
     def out_space(c):
         y_forward(2, c)
@@ -377,53 +373,42 @@
     out_dp(2)
 
     def mix_grad(g):
-        j, base = g // 2, lax.rem(g, 2) * 16
         arrived_dp(2, g)
         widen_dp(2, g, u_ref)
 
         def go(k, carry):
-            rows = pl.ds(k, ND, stride=16)
+            rows = pl.ds(k, ND, stride=M)
             v = u_ref[g, rows, :]
             lhs = jnp.concatenate([v, swap(v) * sign], axis=0)
-            res = dot(lhs.astype(BF16), twice(base + k, j), NT)
+            res = dot(lhs.astype(BF16), twice(k, g), NT)
             m_ref[rows, :] = jnp.where(lo, res[:ND], res[ND:])
             return carry
 
-        lax.fori_loop(0, 16, go, 0, unroll=16)
+        lax.fori_loop(0, M, go, 0, unroll=16)
         narrow_dp(3, g)
         exchange_dp(3, g)
 
-    chunks(mix_grad, 0, 2 * J)
+    chunks(mix_grad)
 
     def weight_grad(g):
-        j, base = g // 2, lax.rem(g, 2) * 16
 
         def go(k, carry):
-            rows = pl.ds(k, ND, stride=16)
+            rows = pl.ds(k, ND, stride=M)
             v = v_ref[g, rows, :]
             grad = u_ref[g, rows, :]
             lhs = jnp.concatenate([v, swap(v)], axis=0).astype(BF16)
             rhs = jnp.concatenate([grad, swap(grad) * sign], axis=0).astype(BF16)
-            gw_ref[base + k, j] = dot(lhs[:, :64], rhs, TN)
+            gw_ref[k, g] = dot(lhs[:, :64], rhs, TN)
             return carry
 
-        lax.fori_loop(0, 16, go, 0, unroll=16)
+        lax.fori_loop(0, M, go, 0, unroll=16)
 
     def back_space_grad(c):
         back_space(3, c)
         weight_grad(c)
 
-    chunks(back_space_grad, 0, 3)
-    back_space(3, 3)
-
-    def back_grid_grad(c):
-        weight_grad(c * 2 + 3)
-        back_grid(3, 0, c)
-        weight_grad(c * 2 + 4)
-
-    chunks(back_grid_grad, 0, 2)
-    weight_grad(7)
-    back_grid(3, 0, 2)
+    chunks(back_space_grad)
+    chunks(lambda c: back_grid(3, 0, c), 0, J - 1)
     arrived_space(3, J - 1)
     y_inverse(3, J - 1)
 
@@ -438,12 +423,22 @@
             pltpu.make_async_copy(part, part, sem_send_d.at[n, g]).wait()
 
         chunks(sent_space)
-        chunks(sent_dp, 0, 2 * J)
+        chunks(sent_dp)
 
 
 def z_part(a_ref, table, q):
     rows = [a_ref[pl.ds(q * 4 + yl, 16, stride=64), :] for yl in range(4)]
     return dot(jnp.concatenate(rows, axis=0).astype(BF16), table, TN)
+
+
+def z_part_pair(a_ref, table, pair):
+    blocks = [
+        jnp.concatenate(
+            [a_ref[pl.ds((pair * 2 + e) * 4 + yl, 16, stride=64), :] for yl in range(4)], axis=0
+        ).astype(BF16)
+        for e in range(2)
+    ]
+    return dot(jnp.concatenate(blocks, axis=1), table, TN)
 
 
 def finish(
@@ -509,17 +504,17 @@
             pltpu.VMEM((LANES, G * G), BF16),
             pltpu.VMEM((4096, LANES), F32),
             pltpu.VMEM((NS * 16, LANES), F32),
-            pltpu.VMEM((2 * J, ND * 16, LANES), F32),
-            pltpu.VMEM((2 * J, ND * 16, LANES), F32),
-            pltpu.VMEM((ND * 16, LANES), F32),
+            pltpu.VMEM((J, ND * M, LANES), F32),
+            pltpu.VMEM((J, ND * M, LANES), F32),
+            pltpu.VMEM((ND * M, LANES), F32),
             pltpu.VMEM((4, J, NS, 16, LANES), BF16),
             pltpu.VMEM((4, J, NS, 16, LANES), BF16),
-            pltpu.VMEM((4, 2 * J, ND, 16, LANES), BF16),
-            pltpu.VMEM((4, 2 * J, ND, 16, LANES), BF16),
+            pltpu.VMEM((4, J, ND, M, LANES), BF16),
+            pltpu.VMEM((4, J, ND, M, LANES), BF16),
             pltpu.SemaphoreType.DMA((4, J)),
             pltpu.SemaphoreType.DMA((4, J)),
-            pltpu.SemaphoreType.DMA((4, 2 * J)),
-            pltpu.SemaphoreType.DMA((4, 2 * J)),
+            pltpu.SemaphoreType.DMA((4, J)),
+            pltpu.SemaphoreType.DMA((4, J)),
             pltpu.SemaphoreType.DMA((7,)),
             pltpu.SemaphoreType.DMA((4,)),
         ],

time: 70.7 us -> 69.7 us (0.986)
  Pallas kernels: 70 us -> 69 us
    pallas_call x1, Pallas kernels: 67.1 us -> 66.1 us  [local(): pl.pallas_call(kernel, out_shape=(pltpu.VMEM(x.shape, BF16), pltpu.VMEM(s...]
where the time goes in v4:
time: 69.7 us; the launch traced here: 69.6 us
  Pallas kernels  69 us (99%)
    pallas_call x1, Pallas kernels, local(): pl.pallas_call(kernel, out_shape=(pltpu.VMEM(x.shape, BF16), pltpu.VMEM(s...  66.1 us
    pallas_call x1, Pallas kernels, local(): pl.pallas_call(finish, out_shape=(jax.ShapeDtypeStruct(x.shape, BF16), ja...  2.91 us

profile of v4, /device:TPU:1, one launch (start us, length us, event | category | flops | bytes accessed | tf_op | source)
XLA Modules:
  0.0 69.6 jit_solution(10289894205790928675)
XLA Ops:
  0.6 66.1 %shard_map.103 = (bf16[128,4096]{1,0:T(8,128)(2,1)S(1)}, f32[32,4,64,128]{3,2,1,0:T(8,128)S(1)}, f32[128,4096]{1,0:T(8,128)S(1)}, f32[1024,128]{1,0:T(8,128)S(1)}, bf16[64,256]{1,0:T(8,128)(2,1)S(1)}) custom-call(bf16[128,4096]{1,0:T(8,128)(2,1)} %bitcast.5, bf16[64,64]{1,0:T(8,128)(2,1)} %weight_hbm.1, f32[1,64]{1,0:T(1,128)} %bitcast.9, ...), custom_call_target="tpu_custom_call" | custom-call | flops 2000000000 | bytes 12582912 | tf_op jit(solution)/shard_map/pallas_call | solution.py:483
  66.7 2.9 %shard_map.104 = (bf16[128,4096]{1,0:T(8,128)(2,1)}, bf16[128,4096]{1,0:T(8,128)(2,1)}, f32[32,4,64,128]{3,2,1,0:T(8,128)}) custom-call(bf16[128,4096]{1,0:T(8,128)(2,1)S(1)} %get-tuple-element.11.out_ref, f32[32,4,64,128]{3,2,1,0:T(8,128)S(1)} %get-tuple-element.12.gw_ref, f32[128,4096]{1,0:T(8,128)S(1)} %get-tuple-element.13.acc_ref, ...), custom_call_target="tpu_custom_call" | custom-call | tf_op jit(solution)/shard_map/pallas_call | solution.py:528

commit v5 on v4

--- a/solution.py
+++ b/solution.py
@@ -172,18 +172,13 @@
         e_ref[pl.ds(pl.multiple_of(q * 256, 256), 256), :] = dot(zf_ref[table], block, NT)
 
     def y_forward(n, c):
-        table = small_ref[0, :64, :]
-        for pair in range(4):
-            parts = [
-                e_ref[pl.ds((pair * 2 + e) * 4 + c, 128, stride=M), :].astype(BF16)
-                for e in range(2)
-            ]
-            res = dot(table, jnp.concatenate(parts, axis=1)).astype(BF16)
-            for e in range(2):
-                for iyl in range(4):
-                    send_s[n, c, iyl * 8 + pair * 2 + e] = res[
-                        iyl * 16 : iyl * 16 + 16, e * 128 : e * 128 + 128
-                    ]
+        parts = [e_ref[pl.ds(izh * 4 + c, 128, stride=M), :].astype(BF16) for izh in range(8)]
+        res = dot(small_ref[0, :64, :], jnp.concatenate(parts, axis=1)).astype(BF16)
+        for izh in range(8):
+            for iyl in range(4):
+                send_s[n, c, iyl * 8 + izh] = res[
+                    iyl * 16 : iyl * 16 + 16, izh * 128 : izh * 128 + 128
+                ]
 
     def x_forward(n_space, n_dp, c):
         f_ref[...] = recv_s[n_space, c].reshape(NS * 16, LANES).astype(F32)
@@ -329,7 +324,7 @@
             m_ref[rows, :] = res[:ND] - swap(res[ND:]) * sign
             return carry
 
-        lax.fori_loop(0, M, go, 0, unroll=16)
+        lax.fori_loop(0, M, go, 0, unroll=32)
         narrow_dp(1, g)
         exchange_dp(1, g)
 
@@ -384,7 +379,7 @@
             m_ref[rows, :] = jnp.where(lo, res[:ND], res[ND:])
             return carry
 
-        lax.fori_loop(0, M, go, 0, unroll=16)
+        lax.fori_loop(0, M, go, 0, unroll=32)
         narrow_dp(3, g)
         exchange_dp(3, g)
 
@@ -454,13 +449,13 @@
         copy.start()
     quarter = G * G // 4
     for i in range(4):
-
-        def last(q, carry):
-            here = pl.ds(pl.multiple_of(q * 256, 256), 256)
-            gin_ref[:, here] = (acc_ref[:, here] + z_part(a_ref, last_ref[...], q)).astype(BF16)
-            return carry
-
-        lax.fori_loop(4 * i, 4 * i + 4, last, 0, unroll=4)
+        for pair in range(2 * i, 2 * i + 2):
+            sums = z_part_pair(a_ref, last_ref[...], pair)
+            for e in range(2):
+                here = pl.ds((pair * 2 + e) * 256, 256)
+                gin_ref[:, here] = (
+                    acc_ref[:, here] + sums[e * 128 : e * 128 + 128]
+                ).astype(BF16)
         part = pl.ds(i * quarter, quarter)
         copy = pltpu.make_async_copy(gin_ref.at[:, part], gin_hbm.at[:, part], sem_gin.at[i])
         copy.start()

time: 69.7 us -> 69.6 us (level)
  no operation moved by 1% of the time
where the time goes in v5:
time: 69.6 us; the launch traced here: 69.5 us
  Pallas kernels  68.8 us (99%)
    pallas_call x1, Pallas kernels, local(): pl.pallas_call(kernel, out_shape=(pltpu.VMEM(x.shape, BF16), pltpu.VMEM(s...  66 us
    pallas_call x1, Pallas kernels, local(): pl.pallas_call(finish, out_shape=(jax.ShapeDtypeStruct(x.shape, BF16), ja...  2.89 us

profile of v5, /device:TPU:1, one launch (start us, length us, event | category | flops | bytes accessed | tf_op | source)
XLA Modules:
  0.0 69.5 jit_solution(3231684477517542509)
XLA Ops:
  0.6 66.0 %shard_map.103 = (bf16[128,4096]{1,0:T(8,128)(2,1)S(1)}, f32[32,4,64,128]{3,2,1,0:T(8,128)S(1)}, f32[128,4096]{1,0:T(8,128)S(1)}, f32[1024,128]{1,0:T(8,128)S(1)}, bf16[64,256]{1,0:T(8,128)(2,1)S(1)}) custom-call(bf16[128,4096]{1,0:T(8,128)(2,1)} %bitcast.5, bf16[64,64]{1,0:T(8,128)(2,1)} %weight_hbm.1, f32[1,64]{1,0:T(1,128)} %bitcast.9, ...), custom_call_target="tpu_custom_call" | custom-call | flops 2000000000 | bytes 12582912 | tf_op jit(solution)/shard_map/pallas_call | solution.py:478
  66.6 2.9 %shard_map.104 = (bf16[128,4096]{1,0:T(8,128)(2,1)}, bf16[128,4096]{1,0:T(8,128)(2,1)}, f32[32,4,64,128]{3,2,1,0:T(8,128)}) custom-call(bf16[128,4096]{1,0:T(8,128)(2,1)S(1)} %get-tuple-element.11.out_ref, f32[32,4,64,128]{3,2,1,0:T(8,128)S(1)} %get-tuple-element.12.gw_ref, f32[128,4096]{1,0:T(8,128)S(1)} %get-tuple-element.13.acc_ref, ...), custom_call_target="tpu_custom_call" | custom-call | tf_op jit(solution)/shard_map/pallas_call | solution.py:523
